TPU v7x, 32 devices: a whole 2x2x4 slice. The times are simulated.
32 devices in a mesh: grp: 4 (over x, core), exp: 8 (over z, y).
Axes of the slice: x: 2, y: 2, z: 4, core: 2. Of those that a mesh axis runs over, the one named last changes fastest.
Arguments:
- tokens: bfloat16 [4096, 2048], P(('grp', 'exp')), may hold values from -6 to 6
- grad_out: bfloat16 [4096, 2048], P(('grp', 'exp')), may hold values from -6 to 6
- probs: bfloat16 [4096, 6], P(('grp', 'exp')), may hold values from 0.049804688 to 0.3984375
- expert_ids: int32 [4096, 6], P(('grp', 'exp')), may hold values from 0 to 15, as said below
- serve_map: int32 [4, 8], replicated, may hold values from 0 to 1, as said below
- replica_pick: int32 [4096, 6], P(('grp', 'exp')), may hold values from 0 to 839
- w_gate: bfloat16 [16, 2048, 768], P('exp'), may hold values from -0.125 to 0.125
- w_up: bfloat16 [16, 2048, 768], P('exp'), may hold values from -0.125 to 0.125
- w_down: bfloat16 [16, 2048, 768], P('exp'), may hold values from -0.21875 to 0.21875
Outputs:
- grad_tokens: bfloat16 [4096, 2048], P(('grp', 'exp'))
- grad_probs: bfloat16 [4096, 6], P(('grp', 'exp'))
- grad_gate: float32 [16, 2048, 768], P('exp', 'grp')
- grad_up: float32 [16, 2048, 768], P('exp', 'grp')
- grad_down: float32 [16, 2048, 768], P('exp', 'grp')
Inputs may be any that keep to these rules, and one draw needn't show every extreme that they name: `serve_map`: entry (g, c) names which of the experts c * 2 + entry the device of group g and column c serves; every expert is served by at least one group. `expert_ids`: each token names 6 different experts.
All inputs are finite; a program needn't handle non-finite values.
Results may differ from a plain program's by a relative error of at most 0.014.
Values may be sent and summed in bfloat16 or wider, within the bound.
No kernel may reach another device: no remote copies, remote signals or barrier semaphores. Data moves between devices by JAX's collectives and lax.ppermute only.
A program may use at most 128 MiB of HBM per device.

v0:
```python
import jax
import jax.numpy as jnp
from jax import lax
from jax.sharding import PartitionSpec as P

EXP_DEV = 2


def route_targets(expert_ids, serve_map, replica_pick):
    groups = serve_map.shape[0]
    columns = serve_map.shape[1]
    column = expert_ids // EXP_DEV
    member = expert_ids % EXP_DEV
    serving = (serve_map[:, column] == member[None]).astype(jnp.int32)
    order_index = jnp.cumsum(serving, axis=0) - 1
    server_count = jnp.sum(serving, axis=0)
    wanted = replica_pick % server_count
    chosen_group = serving * (order_index == wanted[None]).astype(jnp.int32)
    group_index = jnp.sum(chosen_group * jnp.arange(groups, dtype=jnp.int32)[:, None, None], axis=0)
    return group_index * columns + column


def route_ranks(target_flat, devices):
    onehot = (target_flat[:, None] == jnp.arange(devices, dtype=jnp.int32)[None, :]).astype(
        jnp.int32
    )
    running = jnp.cumsum(onehot, axis=0) - onehot
    return jnp.sum(running * onehot, axis=1)


def expert_backward(input_rows, grad_rows, prob_rows, weight_gate, weight_up, weight_down):
    contract = (((1,), (1,)), ((), ()))
    over_rows = (((0,), (0,)), ((), ()))
    gate = jnp.dot(input_rows, weight_gate, preferred_element_type=jnp.float32)
    up_value = jnp.dot(input_rows, weight_up, preferred_element_type=jnp.float32)
    sigmoid_gate = jax.nn.sigmoid(gate)
    silu_gate = gate * sigmoid_gate
    hidden = (silu_gate * up_value).astype(jnp.bfloat16)
    output = lax.dot_general(hidden, weight_down, contract, preferred_element_type=jnp.float32)
    route_prob = jnp.sum(grad_rows.astype(jnp.float32) * output, axis=1).astype(jnp.bfloat16)
    scaled = (prob_rows.astype(jnp.float32)[:, None] * grad_rows.astype(jnp.float32)).astype(
        jnp.bfloat16
    )
    grad_hidden = jnp.dot(scaled, weight_down, preferred_element_type=jnp.float32)
    grad_gate_pre = (
        grad_hidden * up_value * sigmoid_gate * (1.0 + gate * (1.0 - sigmoid_gate))
    ).astype(jnp.bfloat16)
    grad_up_pre = (grad_hidden * silu_gate).astype(jnp.bfloat16)
    route_grad = lax.dot_general(
        grad_gate_pre, weight_gate, contract, preferred_element_type=jnp.float32
    )
    route_grad = (
        route_grad
        + lax.dot_general(grad_up_pre, weight_up, contract, preferred_element_type=jnp.float32)
    ).astype(jnp.bfloat16)
    part_gate = lax.dot_general(
        input_rows, grad_gate_pre, over_rows, preferred_element_type=jnp.float32
    ).astype(jnp.bfloat16)
    part_up = lax.dot_general(
        input_rows, grad_up_pre, over_rows, preferred_element_type=jnp.float32
    ).astype(jnp.bfloat16)
    part_down = lax.dot_general(
        scaled, hidden, over_rows, preferred_element_type=jnp.float32
    ).astype(jnp.bfloat16)
    return (route_grad, route_prob, part_gate, part_up, part_down)


def body(tokens, grad_out, probs, expert_ids, serve_map, replica_pick, w_gate, w_up, w_down):
    groups = lax.axis_size("grp")
    columns = lax.axis_size("exp")
    devices = groups * columns
    local_tokens, chosen = expert_ids.shape
    model_width = tokens.shape[1]
    capacity = local_tokens * chosen * 4 // (3 * devices)
    buffer_rows = devices * capacity
    target = route_targets(expert_ids, serve_map, replica_pick)
    slot_rank = route_ranks(target.reshape(-1), devices).reshape(local_tokens, chosen)
    kept_mask = slot_rank < capacity
    route_slot = target * capacity + slot_rank
    send_slot = jnp.where(kept_mask, route_slot, buffer_rows)
    route_id = jnp.arange(local_tokens * chosen, dtype=jnp.int32)
    slot_table = (
        jnp.full((buffer_rows,), -1, jnp.int32).at[send_slot.reshape(-1)].set(route_id, mode="drop")
    )
    live_mask = slot_table >= 0
    safe_slot = jnp.where(live_mask, slot_table, 0)
    token_row = safe_slot // chosen
    input_send = jnp.where(live_mask[:, None], tokens[token_row], jnp.zeros((), jnp.bfloat16))
    grad_send = jnp.where(live_mask[:, None], grad_out[token_row], jnp.zeros((), jnp.bfloat16))
    prob_send = jnp.where(live_mask, probs.reshape(-1)[safe_slot], jnp.zeros((), jnp.bfloat16))
    input_rows, grad_rows, prob_rows = (
        lax.all_to_all(
            input_send.reshape(devices, capacity, model_width),
            ("grp", "exp"),
            split_axis=0,
            concat_axis=0,
            tiled=True,
        ),
        lax.all_to_all(
            grad_send.reshape(devices, capacity, model_width),
            ("grp", "exp"),
            split_axis=0,
            concat_axis=0,
            tiled=True,
        ),
        lax.all_to_all(
            prob_send.reshape(devices, capacity),
            ("grp", "exp"),
            split_axis=0,
            concat_axis=0,
            tiled=True,
        ),
    )
    input_rows = input_rows.reshape(buffer_rows, model_width)
    grad_rows = grad_rows.reshape(buffer_rows, model_width)
    prob_rows = prob_rows.reshape(buffer_rows)
    group_index = lax.axis_index("grp")
    column = lax.axis_index("exp")
    served = serve_map[group_index, column]
    weight_gate = lax.dynamic_index_in_dim(w_gate, served, 0, keepdims=False)
    weight_up = lax.dynamic_index_in_dim(w_up, served, 0, keepdims=False)
    weight_down = lax.dynamic_index_in_dim(w_down, served, 0, keepdims=False)
    route_grad, route_prob, part_gate, part_up, part_down = expert_backward(
        input_rows, grad_rows, prob_rows, weight_gate, weight_up, weight_down
    )
    grad_back, prob_back = (
        lax.all_to_all(
            route_grad.reshape(devices, capacity, model_width),
            ("grp", "exp"),
            split_axis=0,
            concat_axis=0,
            tiled=True,
        ),
        lax.all_to_all(
            route_prob.reshape(devices, capacity),
            ("grp", "exp"),
            split_axis=0,
            concat_axis=0,
            tiled=True,
        ),
    )
    grad_back = grad_back.reshape(buffer_rows, model_width)
    prob_back = prob_back.reshape(buffer_rows)
    read_slot = jnp.where(kept_mask, route_slot, 0)
    routed = jnp.where(kept_mask[:, :, None], grad_back[read_slot], jnp.zeros((), jnp.bfloat16))
    grad_tokens = jnp.sum(routed.astype(jnp.float32), axis=1).astype(jnp.bfloat16)
    grad_probs = jnp.where(kept_mask, prob_back[read_slot], jnp.zeros((), jnp.bfloat16))
    slot_flag = (jnp.arange(EXP_DEV, dtype=jnp.int32) == served)[:, None, None]

    def spread(partial_value):
        return jnp.where(slot_flag, partial_value.astype(jnp.float32)[None], 0.0)

    grad_gate, grad_up, grad_down = (
        lax.psum_scatter(
            spread(part_gate).astype(jnp.bfloat16), "grp", scatter_dimension=1, tiled=True
        ).astype(jnp.float32),
        lax.psum_scatter(
            spread(part_up).astype(jnp.bfloat16), "grp", scatter_dimension=1, tiled=True
        ).astype(jnp.float32),
        lax.psum_scatter(
            spread(part_down).astype(jnp.bfloat16), "grp", scatter_dimension=1, tiled=True
        ).astype(jnp.float32),
    )
    return (grad_tokens, grad_probs, grad_gate, grad_up, grad_down)


def solution(mesh):
    in_specs = (
        P(("grp", "exp"), None),
        P(("grp", "exp"), None),
        P(("grp", "exp"), None),
        P(("grp", "exp"), None),
        P(),
        P(("grp", "exp"), None),
        P("exp", None, None),
        P("exp", None, None),
        P("exp", None, None),
    )
    out_specs = (
        P(("grp", "exp"), None),
        P(("grp", "exp"), None),
        P("exp", "grp", None),
        P("exp", "grp", None),
        P("exp", "grp", None),
    )
    return jax.shard_map(body, mesh=mesh, in_specs=in_specs, out_specs=out_specs, check_vma=False)
```

profile of v0, /device:TPU:0, one launch (start us, length us, event | category | flops | bytes accessed | tf_op | source)
XLA Modules:
  0.0 515.5 jit_solution(9568780022227982050)
XLA Ops:
  19.1 6.8 %gather_fusion.1 = bf16[1024]{0:T(1024)(128)(2,1)S(1)} fusion(bf16[768]{0:T(1024)(128)(2,1)S(1)} %reshape.148, s32[1024]{0:T(1024)S(1)} %get-tuple-element.22), kind=kCustom, calls=%fused_computation.1 | custom fusion | bytes 8192 | tf_op jit(solution)/shard_map/gather | solution.py:90
  26.6 7.3 %all-to-all-start = ((bf16[32,1,32]{2,1,0:T(2,128)(2,1)}), bf16[32,1,32]{2,1,0:T(2,128)(2,1)S(1)}, u32[]{:S(2)}, u32[]{:S(2)}) async-start(bf16[32,1,32]{2,1,0:T(2,128)(2,1)} %all_to_all.25), calls=%async_computation | async-start | bytes 32768 | tf_op jit(solution)/shard_map/all_to_all | solution.py:106
  34.0 6.0 %gather_fusion.3 = bf16[1024,2048]{1,0:T(8,128)(2,1)} fusion(bf16[128,2048]{1,0:T(8,128)(2,1)S(1)} %copy-done, s32[1024]{0:T(1024)S(1)} %fusion.33), kind=kCustom, calls=%fused_computation.3 | custom fusion | bytes 8392704 | tf_op jit(solution)/shard_map/gather | solution.py:88
  40.0 6.1 %gather_fusion.2 = bf16[1024,2048]{1,0:T(8,128)(2,1)} fusion(bf16[128,2048]{1,0:T(8,128)(2,1)S(1)} %copy-done.2, s32[1024]{0:T(1024)S(1)} %fusion.33), kind=kCustom, calls=%fused_computation.2 | custom fusion | bytes 8392704 | tf_op jit(solution)/shard_map/gather | solution.py:89
  46.1 5.8 %broadcast_select_fusion.1 = (bf16[32,32,2048]{2,1,0:T(8,128)(2,1)}, bf16[32,32,2048]{2,1,0:T(8,128)(2,1)}) fusion(bf16[32,32,2048]{2,1,0:T(8,128)(2,1)} %bitcast.74, pred[32,32]{1,0:T(8,128)(4,1)S(1)} %broadcast_in_dim.121, bf16[32,32,2048]{2,1,0:T(8,128)(2,1)} %bitcast.73), kind=kLoop, calls=%fused_computation.19 | loop fusion | flops 4194304 | bytes 16778240 | tf_op jit(solution)/shard_map/jit(_where)/select_n | solution.py:89
  51.9 100.9 %all_to_all.31 = bf16[32,32,2048]{2,1,0:T(8,128)(2,1)} all-to-all(bf16[32,32,2048]{2,1,0:T(8,128)(2,1)} %get-tuple-element.30), channel_id=1, replica_groups=mesh['grp'=4,'exp'=8] {'grp','exp'}, dimensions={0} | all-to-all | bytes 8388608 | tf_op jit(solution)/shard_map/all_to_all | solution.py:92
  160.7 8.2 %fusion.8 = f32[1024,768]{1,0:T(8,128)} fusion(bf16[1024,2048]{1,0:T(8,128)(2,1)} %bitcast.75, bf16[2,2048,768]{2,1,0:T(8,128)(2,1)} %param.15, s32[]{:T(128)S(6)} %select_n.118), kind=kOutput, calls=%fused_computation.28 | convolution fusion | flops 3221225472 | bytes 10485764 | tf_op jit(solution)/shard_map/dot_general | solution.py:34
  168.9 83.5 %all-to-all-done.1 = bf16[32,32,2048]{2,1,0:T(8,128)(2,1)} async-done(((bf16[32,32,2048]{2,1,0:T(8,128)(2,1)}), bf16[32,32,2048]{2,1,0:T(8,128)(2,1)}, u32[]{:S(2)}, u32[]{:S(2)}) %all-to-all-start.1) | async-done | bytes 4194336 | tf_op jit(solution)/shard_map/all_to_all | solution.py:99
  255.5 5.5 %fusion.14 = f32[1024,768]{1,0:T(8,128)S(1)} fusion(bf16[1024,2048]{1,0:T(8,128)(2,1)S(1)} %bitcast.80, bf16[2,2048,768]{2,1,0:T(8,128)(2,1)} %param.17, s32[]{:T(128)S(6)} %select_n.118), kind=kOutput, calls=%fused_computation.34 | convolution fusion | flops 3221225472 | bytes 10485764 | tf_op jit(solution)/shard_map/dot_general | solution.py:44
  261.0 4.5 multiply_convert_fusion
  265.5 4.0 fusion.5
  269.6 3.8 fusion.4
  276.4 3.8 fusion.3
  280.2 7.6 %select_convert_fusion = (bf16[2,2048,768]{2,1,0:T(8,128)(2,1)}, bf16[2,2048,768]{2,1,0:T(8,128)(2,1)}, bf16[2,2048,768]{2,1,0:T(8,128)(2,1)}) fusion(bf16[2048,768]{1,0:T(8,128)(2,1)S(1)} %fusion.3, pred[2]{0:T(512)(128)(4,1)S(1)} %iota_compare_fusion.2, bf16[2048,768]{1,0:T(8,128)(2,1)S(1)} %fusion.4, bf16[2048,768]{1,0:T(8,128)(2,1)S(1)} %fusion.5), kind=kLoop, calls=%fused_computation.7 | loop fusion | flops 9437184 | bytes 28311554 | tf_op jit(solution)/shard_map/convert_element_type | solution.py:161
  289.3 8.7 %fusion.1 = bf16[1024]{0:T(1024)(128)(2,1)S(1)} fusion(bf16[32,32,2048]{2,1,0:T(8,128)(2,1)} %all-to-all-done.1, bf16[1024,768]{1,0:T(8,128)(2,1)} %copy-done.8, bf16[2,2048,768]{2,1,0:T(8,128)(2,1)} %param.17, s32[]{:T(128)S(6)} %select_n.118), kind=kOutput, calls=%fused_computation.14 | convolution fusion | flops 3227515904 | bytes 8914948 | tf_op jit(solution)/shard_map/dot_general | solution.py:39
  301.5 5.5 %fusion.6 = f32[1024,2048]{1,0:T(8,128)S(1)} fusion(bf16[1024,768]{1,0:T(8,128)(2,1)S(1)} %get-tuple-element.27, bf16[2,2048,768]{2,1,0:T(8,128)(2,1)} %param.15, s32[]{:T(128)S(6)} %select_n.118), kind=kOutput, calls=%fused_computation.26 | convolution fusion | flops 3221225472 | bytes 13107204 | tf_op jit(solution)/shard_map/dot_general | solution.py:49
  306.9 7.1 %add_convert_fusion = bf16[1024,2048]{1,0:T(8,128)(2,1)} fusion(f32[1024,2048]{1,0:T(8,128)S(1)} %fusion.6, bf16[1024,768]{1,0:T(8,128)(2,1)S(1)} %copy-done.7, bf16[2,2048,768]{2,1,0:T(8,128)(2,1)} %param.16, s32[]{:T(128)S(6)} %select_n.118), kind=kOutput, calls=%fused_computation.16 | convolution fusion | flops 3225419776 | bytes 17301508 | tf_op jit(solution)/shard_map/dot_general | solution.py:54
  314.1 6.1 %all-to-all-start.3 = ((bf16[32,32,2048]{2,1,0:T(8,128)(2,1)}), bf16[32,32,2048]{2,1,0:T(8,128)(2,1)}, u32[]{:S(2)}, u32[]{:S(2)}) async-start(bf16[32,32,2048]{2,1,0:T(8,128)(2,1)} %bitcast.79), calls=%async_computation.3 | async-start | bytes 8388608 | tf_op jit(solution)/shard_map/all_to_all | solution.py:127
  320.7 5.0 gather_fusion.5
  326.5 89.6 %all-to-all-done.3 = bf16[32,32,2048]{2,1,0:T(8,128)(2,1)} async-done(((bf16[32,32,2048]{2,1,0:T(8,128)(2,1)}), bf16[32,32,2048]{2,1,0:T(8,128)(2,1)}, u32[]{:S(2)}, u32[]{:S(2)}) %all-to-all-start.3) | async-done | bytes 4194336 | tf_op jit(solution)/shard_map/all_to_all | solution.py:127
  416.1 9.1 %gather_fusion.4 = bf16[768,2048]{1,0:T(8,128)(2,1)S(1)} fusion(bf16[1024,2048]{1,0:T(8,128)(2,1)} %bitcast.12, s32[1024]{0:T(1024)S(1)} %pad_clamp_fusion), kind=kCustom, calls=%fused_computation.4 | custom fusion | bytes 6294528 | tf_op jit(solution)/shard_map/gather | solution.py:145
  428.1 5.4 %select_reduce_fusion = bf16[128,2048]{1,0:T(8,128)(2,1)} fusion(bf16[128,6,2048]{2,1,0:T(8,128)(2,1)} %reshape.189, pred[128,6]{1,0:T(8,128)(4,1)S(1)} %copy.80), kind=kLoop, calls=%fused_computation.17 | loop fusion | flops 2883584 | bytes 3670784 | tf_op jit(solution)/shard_map/reduce_sum | solution.py:146
  436.8 9.0 %reduce-scatter.6.cloned.1.call-done = bf16[2,512,768]{2,1,0:T(8,128)(2,1)} async-done(((bf16[2,2048,768]{2,1,0:T(8,128)(2,1)}), bf16[2,512,768]{2,1,0:T(8,128)(2,1)}) %reduce-scatter.6.cloned.1.call-update) | async-done | bytes 1572880 | tf_op jit(solution)/shard_map/reduce_scatter | solution.py:157
  449.1 56.1 %reduce-scatter.8.cloned.1.call-done = bf16[2,512,768]{2,1,0:T(8,128)(2,1)} async-done(((bf16[2,2048,768]{2,1,0:T(8,128)(2,1)}), bf16[2,512,768]{2,1,0:T(8,128)(2,1)}) %reduce-scatter.8.cloned.1.call-update) | async-done | bytes 1572880 | tf_op jit(solution)/shard_map/reduce_scatter | solution.py:160
  (97 shorter events, 43.6 us)
Async XLA Ops:
  7.2 26.8 %copy-start = (bf16[128,2048]{1,0:T(8,128)(2,1)S(1)}, bf16[128,2048]{1,0:T(8,128)(2,1)}, u32[]{:S(2)}) copy-start(bf16[128,2048]{1,0:T(8,128)(2,1)} %param.9) | copy-start | bytes 1572868
  7.2 5.1 copy-start.4
  7.2 5.5 %copy-start.5 = (bf16[128,6]{0,1:T(8,128)(2,1)S(1)}, bf16[128,6]{0,1:T(8,128)(2,1)}, u32[]{:S(2)}) copy-start(bf16[128,6]{0,1:T(8,128)(2,1)} %param.11) | copy-start | bytes 4612
  26.6 25.3 %all-to-all-start = ((bf16[32,1,32]{2,1,0:T(2,128)(2,1)}), bf16[32,1,32]{2,1,0:T(2,128)(2,1)S(1)}, u32[]{:S(2)}, u32[]{:S(2)}) async-start(bf16[32,1,32]{2,1,0:T(2,128)(2,1)} %all_to_all.25), calls=%async_computation | async-start | bytes 32768 | tf_op jit(solution)/shard_map/all_to_all | solution.py:106
  34.0 6.0 %copy-start.2 = (bf16[128,2048]{1,0:T(8,128)(2,1)S(1)}, bf16[128,2048]{1,0:T(8,128)(2,1)}, u32[]{:S(2)}) copy-start(bf16[128,2048]{1,0:T(8,128)(2,1)} %param.10) | copy-start | bytes 1572868
  152.8 99.5 %all-to-all-start.1 = ((bf16[32,32,2048]{2,1,0:T(8,128)(2,1)}), bf16[32,32,2048]{2,1,0:T(8,128)(2,1)}, u32[]{:S(2)}, u32[]{:S(2)}) async-start(bf16[32,32,2048]{2,1,0:T(8,128)(2,1)} %get-tuple-element.29), calls=%async_computation.1 | async-start | bytes 8388608 | tf_op jit(solution)/shard_map/all_to_all | solution.py:99
  156.4 277.0 %reduce-scatter.4.cloned.1.call-start = ((), (), s32[]{:S(2)}) async-start(), calls=%async_computation.8 | async-start | bytes 7864320 | tf_op jit(solution)/shard_map/reduce_scatter | solution.py:154
  252.4 8.6 %slice-start = ((s8[6291456]{0:T(1024)(128)(4,1)}), s8[4194304]{0:T(1024)(128)(4,1)S(1)}, s32[]{:S(2)}) async-start(s8[6291456]{0:T(1024)(128)(4,1)} %bitcast.83), calls=%async_computation.11 | async-start | bytes 8388608
  255.5 5.5 %copy-start.3 = (bf16[32,32,2048]{2,1,0:T(8,128)(2,1)S(1)}, bf16[32,32,2048]{2,1,0:T(8,128)(2,1)}, u32[]{:S(2)}) copy-start(bf16[32,32,2048]{2,1,0:T(8,128)(2,1)} %all_to_all.31) | copy-start | bytes 12582916
  255.5 5.5 %slice-start.1 = ((s8[6291456]{0:T(1024)(128)(4,1)}), s8[2097152]{0:T(1024)(128)(4,1)S(1)}, s32[]{:S(2)}) async-start(s8[6291456]{0:T(1024)(128)(4,1)} %bitcast.83), calls=%async_computation.12 | async-start | bytes 4194304
  255.5 5.5 %copy-start.9 = (f32[1024,768]{1,0:T(8,128)S(1)}, f32[1024,768]{1,0:T(8,128)}, u32[]{:S(2)}) copy-start(f32[1024,768]{1,0:T(8,128)} %fusion.8) | copy-start | bytes 9437188
  265.5 4.1 copy-start.6
  265.5 10.8 %copy-start.8 = (bf16[1024,768]{1,0:T(8,128)(2,1)}, bf16[1024,768]{1,0:T(8,128)(2,1)S(1)}, u32[]{:S(2)}) copy-start(bf16[1024,768]{1,0:T(8,128)(2,1)S(1)} %get-tuple-element.26) | copy-start | bytes 4718596
  287.8 158.0 %reduce-scatter.6.cloned.1.call-start = ((), (), s32[]{:S(2)}) async-start(), calls=%async_computation.9 | async-start | bytes 7864320 | tf_op jit(solution)/shard_map/reduce_scatter | solution.py:157
  288.6 216.7 %reduce-scatter.8.cloned.1.call-start = ((), (), s32[]{:S(2)}) async-start(), calls=%async_computation.10 | async-start | bytes 7864320 | tf_op jit(solution)/shard_map/reduce_scatter | solution.py:160
  298.7 15.4 %all-to-all-start.4 = ((bf16[32,1,32]{2,1,0:T(2,128)(2,1)}), bf16[32,1,32]{2,1,0:T(2,128)(2,1)S(1)}, u32[]{:S(2)}, u32[]{:S(2)}) async-start(bf16[32,1,32]{2,1,0:T(2,128)(2,1)} %convert_element_type.144), calls=%async_computation.4 | async-start | bytes 32768 | tf_op jit(solution)/shard_map/all_to_all | solution.py:134
  301.5 5.5 %copy-start.7 = (bf16[1024,768]{1,0:T(8,128)(2,1)S(1)}, bf16[1024,768]{1,0:T(8,128)(2,1)}, u32[]{:S(2)}) copy-start(bf16[1024,768]{1,0:T(8,128)(2,1)} %copy-done.6) | copy-start | bytes 4718596
  314.1 102.0 %all-to-all-start.3 = ((bf16[32,32,2048]{2,1,0:T(8,128)(2,1)}), bf16[32,32,2048]{2,1,0:T(8,128)(2,1)}, u32[]{:S(2)}, u32[]{:S(2)}) async-start(bf16[32,32,2048]{2,1,0:T(8,128)(2,1)} %bitcast.79), calls=%async_computation.3 | async-start | bytes 8388608 | tf_op jit(solution)/shard_map/all_to_all | solution.py:127
  433.4 75.1 %copy-start.1 = (bf16[128,2048]{1,0:T(8,128)(2,1)S(1)}, bf16[128,2048]{1,0:T(8,128)(2,1)}, u32[]{:S(2)}) copy-start(bf16[128,2048]{1,0:T(8,128)(2,1)} %param.9) | copy-start | bytes 1572868
Sparse Core Ops, SparseCore 0:
  287.9 90.9 reduce-scatter.3
  381.6 64.1 reduce-scatter.5
  448.3 56.8 reduce-scatter.7
where the time goes:
time: 520 us; the launch traced here: 516 us
  waiting for transfers between devices  240 us (46%)
  blocking collectives  101 us (19%)
  matrix products  51.2 us (10%)
  local copies, waits for them, and re-layouts  47.4 us (9%)
  other arithmetic  39.8 us (8%)
  starting transfers between devices  20 us (4%)
  between operations  16.6 us (3%)
    all_to_all x1, blocking collectives, body(): lax.all_to_all(input_send.reshape(devices, capacity, model_width), ('grp'...  101 us
    all_to_all x1, waiting for transfers between devices, body(): lax.all_to_all(route_grad.reshape(devices, capacity, model_width), ('grp'...  89.6 us
    all_to_all x1, waiting for transfers between devices, body(): lax.all_to_all(grad_send.reshape(devices, capacity, model_width), ('grp',...  83.5 us
    reduce_scatter x1, waiting for transfers between devices, body(): lax.psum_scatter(spread(part_down).astype(jnp.bfloat16), 'grp', scatter_d...  56.1 us
    gather x2, local copies, waits for them, and re-layouts, body(): grad_back[read_slot]  11.9 us
  transfers between devices with their start and end apart: 7, of which 4 were waited for; matrix products, arithmetic and copies ran while one was open for 16% of the time, Pallas kernels for 0%

commit v1 on v0

v1 whole, which is shorter than its diff:
```python
import functools

import jax
import jax.numpy as jnp
from jax import lax
from jax.experimental import pallas as pl
from jax.experimental.pallas import tpu as pltpu
from jax.sharding import PartitionSpec as P

EXP_DEV = 2
BF = jnp.bfloat16
F32 = jnp.float32


VMEM_BYTES = 56 * 2**20
ANY = pl.BlockSpec(memory_space=pl.ANY)


def dot(a, b, ca, cb):
    return lax.dot_general(a, b, (((ca,), (cb,)), ((), ())), preferred_element_type=F32)


def routing(probs, expert_ids, serve_map, replica_pick, capacity):
    groups, columns = serve_map.shape
    devices = groups * columns
    tokens = expert_ids.shape[0]
    member_of = serve_map.reshape(devices)
    serves_expert = 2 * (jnp.arange(devices, dtype=jnp.int32) % columns) + member_of
    same = (serve_map[:, None, :] == serve_map[None, :, :]).astype(jnp.int32)
    earlier = jnp.tril(jnp.ones((groups, groups), jnp.int32), -1)
    place = jnp.sum(same * earlier[:, :, None], axis=1).reshape(devices)
    count = jnp.sum(same, axis=1).reshape(devices)
    hit = (expert_ids[:, :, None] == serves_expert[None, None, :]) & (
        lax.rem(replica_pick[:, :, None], count[None, None, :]) == place[None, None, :]
    )
    chosen = jnp.sum(hit.astype(F32), axis=1)
    before = jnp.tril(jnp.ones((tokens, tokens), BF), -1)
    rank = dot(before, chosen.astype(BF), 1, 0)
    kept = (rank < capacity) & (chosen > 0)
    prob_dest = jnp.sum(jnp.where(hit, probs.astype(F32)[:, :, None], 0.0), axis=1)
    prob_dest = jnp.where(kept, prob_dest, 0.0).reshape(tokens, groups, columns)
    member = jnp.arange(EXP_DEV, dtype=jnp.int32)
    serving = (serve_map[:, :, None] == member[None, None, :]).astype(F32)
    prob_expert = jnp.sum(prob_dest[:, :, :, None] * serving[None], axis=1)
    kept_route = jnp.sum(jnp.where(hit & kept[:, None, :], 1.0, 0.0), axis=2) > 0
    return prob_expert, kept_route


def fetch(pieces, dst, sem, columns=None, at=0):
    copies = []
    row = 0
    for i, piece in enumerate(pieces):
        n = piece.shape[0]
        src = piece if columns is None else piece.at[:, columns]
        width = src.shape[1]
        copies.append(
            pltpu.make_async_copy(src, dst.at[pl.ds(row, n), pl.ds(at, width)], sem.at[i])
        )
        row += n
    for c in copies:
        c.start()
    return copies


def params(grid):
    return dict(
        compiler_params=pltpu.CompilerParams(
            vmem_limit_bytes=VMEM_BYTES, dimension_semantics=("arbitrary",) * grid
        )
    )


def cost(flops, nbytes, trans=0):
    return pl.CostEstimate(flops=int(flops), bytes_accessed=int(nbytes), transcendentals=int(trans))


def hidden_kernel(count, nb, *refs):
    pieces = refs[:count]
    wg, wu, hid, act, silu_out, x, sem = refs[count:]

    @pl.when(pl.program_id(0) == 0)
    def _():
        for c in fetch(pieces, x, sem):
            c.wait()

    for j in range(0, wg.shape[2], nb):
        cols = slice(j, j + nb)
        gate = jnp.dot(x[...], wg[0, :, cols], preferred_element_type=F32)
        up = jnp.dot(x[...], wu[0, :, cols], preferred_element_type=F32)
        sig = 1.0 / (1.0 + jnp.exp(-gate))
        silu = gate * sig
        hid[:, cols] = (silu * up).astype(BF)
        act[:, cols] = (up * sig * (1.0 + gate * (1.0 - sig))).astype(BF)
        silu_out[:, cols] = silu.astype(BF)


def hidden_call(pieces, w_gate, w_up, nb=256):
    rows = sum(a.shape[0] for a in pieces)
    n, width, ff = w_gate.shape
    ob = pl.BlockSpec((rows, ff), lambda m: (0, m))
    os = jax.ShapeDtypeStruct((rows, n * ff), BF)
    wb = pl.BlockSpec((1, width, ff), lambda m: (m, 0, 0))
    return pl.pallas_call(
        functools.partial(hidden_kernel, len(pieces), nb),
        grid=(n,),
        in_specs=[ANY] * len(pieces) + [wb, wb],
        out_specs=[ob] * 3,
        out_shape=[os] * 3,
        scratch_shapes=[pltpu.VMEM((rows, width), BF), pltpu.SemaphoreType.DMA((len(pieces),))],
        cost_estimate=cost(4 * rows * width * n * ff, 4 * n * width * ff + 8 * rows * ff * n),
        name="hidden",
        **params(1),
    )(*pieces, w_gate, w_up)


def back_kernel(counts, row_counts, planes, nb, plane_ref, *refs):
    na, nn = counts
    pa, pb = refs[:na], refs[na : na + nn]
    refs = refs[na + nn :]
    wd, p = refs[0], refs[1]
    k = len(row_counts)
    hid, act, silu = refs[2 : 2 + k], refs[2 + k : 2 + 2 * k], refs[2 + 2 * k : 2 + 3 * k]
    gg, gu, pg, g, sem, sem2 = refs[2 + 3 * k :]
    m = pl.program_id(0)
    w = g.shape[1] // planes

    @pl.when(m == 0)
    def _():
        one = fetch(pa, g, sem)
        two = fetch(pb, g, sem2, at=g.shape[1] - w)
        for c in one + two:
            c.wait()
        pg[...] = jnp.zeros_like(pg)

    row = 0
    for i, n in enumerate(row_counts):
        here = slice(row, row + n)
        pv = jnp.where(m == 0, p[here, 0:1], p[here, 1:2])
        total = jnp.zeros((n, 1), F32)
        for j in range(0, wd.shape[3], nb):
            cols = slice(j, j + nb)
            back = jnp.zeros((n, nb), F32)
            for s in range(planes):
                at = lax.rem(plane_ref[0] + 1 + s, planes)
                back += jnp.dot(
                    g[here, s * w : (s + 1) * w], wd[0, at, :, cols], preferred_element_type=F32
                )
            total += jnp.sum(back * hid[i][:, cols].astype(F32), axis=1, keepdims=True)
            back = back * pv
            gg[here, cols] = (back * act[i][:, cols]).astype(BF)
            gu[here, cols] = (back * silu[i][:, cols]).astype(BF)
        lane = lax.broadcasted_iota(jnp.int32, (n, pg.shape[1]), 1) == m
        pg[here, :] += jnp.where(lane, total, 0.0)
        row += n


def back_call(plane, pa, pb, w_down, p, hid, act, silu, planes, nb=256):
    rows = sum(a.shape[0] for a in pa)
    n, width, ff = w_down.shape
    w = width // planes
    row_counts = [a.shape[0] for a in hid]
    ob = pl.BlockSpec((rows, ff), lambda m, *_: (0, m))
    os = jax.ShapeDtypeStruct((rows, n * ff), BF)
    acts = [pl.BlockSpec((r, ff), lambda m, *_: (0, m)) for r in row_counts]
    wb = pl.BlockSpec((1, planes, w, ff), lambda m, *_: (m, 0, 0, 0))
    return pl.pallas_call(
        functools.partial(back_kernel, (len(pa), len(pb)), row_counts, planes, nb),
        grid_spec=pltpu.PrefetchScalarGridSpec(
            num_scalar_prefetch=1,
            grid=(n,),
            in_specs=[ANY] * (len(pa) + len(pb))
            + [wb, pl.BlockSpec((rows, n), lambda m, *_: (0, 0))]
            + acts * 3,
            out_specs=[ob, ob, pl.BlockSpec((rows, n), lambda m, *_: (0, 0))],
            scratch_shapes=[
                pltpu.VMEM((rows, width), BF),
                pltpu.SemaphoreType.DMA((len(pa),)),
                pltpu.SemaphoreType.DMA((len(pb),)),
            ],
        ),
        out_shape=[os, os, jax.ShapeDtypeStruct((rows, n), F32)],
        cost_estimate=cost(2 * rows * width * n * ff, 2 * n * width * ff + 14 * rows * ff * n),
        name="back",
        **params(1),
    )(plane, *pa, *pb, w_down.reshape(n, planes, w, ff), p, *hid, *act, *silu)


def part_kernel(count, row_counts, arrays, scale, start_ref, *refs):
    pieces = refs[:count]
    refs = refs[count:]
    if scale:
        p, refs = refs[0], refs[1:]
    k = len(row_counts)
    rhs = [refs[i * k : (i + 1) * k] for i in range(arrays)]
    refs = refs[arrays * k :]
    out, lhs, sem = refs
    block = lhs.shape[1]
    m = pl.program_id(0)

    @pl.when(m == 0)
    def _():
        cols = pl.ds(pl.multiple_of(start_ref[0] * 128, 128), block)
        for c in fetch(pieces, lhs, sem, columns=cols):
            c.wait()

    for i in range(arrays):
        total = None
        row = 0
        for j, n in enumerate(row_counts):
            r = rhs[i][j][...]
            if scale:
                here = slice(row, row + n)
                pv = jnp.where(m == 0, p[here, 0:1], p[here, 1:2])
                r = (r.astype(F32) * pv).astype(BF)
            t = lax.dot_general(
                lhs[row : row + n, :], r, (((0,), (0,)), ((), ())), preferred_element_type=F32
            )
            total = t if total is None else total + t
            row += n
        out[i, 0] = total.astype(BF)


def part_call(start, block, pieces, rhs, p=None):
    rows = sum(a.shape[0] for a in pieces)
    n = EXP_DEV
    k = len(rhs)
    ff = rhs[0][0].shape[1] // n
    row_counts = [a.shape[0] for a in rhs[0]]
    ob = pl.BlockSpec((k, 1, block, ff), lambda m, *_: (0, m, 0, 0))
    scale = [] if p is None else [p]
    flat_rhs = [a for r in rhs for a in r]
    return pl.pallas_call(
        functools.partial(part_kernel, len(pieces), row_counts, k, bool(scale)),
        grid_spec=pltpu.PrefetchScalarGridSpec(
            num_scalar_prefetch=1,
            grid=(n,),
            in_specs=[ANY] * len(pieces)
            + [pl.BlockSpec((rows, n), lambda m, *_: (0, 0))] * len(scale)
            + [pl.BlockSpec((r, ff), lambda m, *_: (0, m)) for r in row_counts] * k,
            out_specs=ob,
            scratch_shapes=[
                pltpu.VMEM((rows, block), BF),
                pltpu.SemaphoreType.DMA((len(pieces),)),
            ],
        ),
        out_shape=jax.ShapeDtypeStruct((k, n, block, ff), BF),
        cost_estimate=cost(
            2 * rows * block * n * ff * k,
            2 * rows * (block + k * n * ff) + 4 * k * n * block * ff,
        ),
        name="part",
        **params(1),
    )((start // 128).astype(jnp.int32).reshape(1), *pieces, *scale, *flat_rhs)


def input_kernel(gg, gu, wg, wu, out):
    ff = wg.shape[2]
    c = (((1,), (1,)), ((), ()))
    acc = lax.dot_general(gg[:, :ff], wg[0], c, preferred_element_type=F32)
    acc += lax.dot_general(gg[:, ff:], wg[1], c, preferred_element_type=F32)
    acc += lax.dot_general(gu[:, :ff], wu[0], c, preferred_element_type=F32)
    acc += lax.dot_general(gu[:, ff:], wu[1], c, preferred_element_type=F32)
    out[...] = acc.astype(BF)


def input_call(gg, gu, w_gate, w_up, nb=512):
    rows = gg.shape[0]
    n, width, ff = w_gate.shape
    wb = pl.BlockSpec((n, nb, ff), lambda j: (0, j, 0))
    gb = pl.BlockSpec((rows, n * ff), lambda j: (0, 0))
    return pl.pallas_call(
        input_kernel,
        grid=(width // nb,),
        in_specs=[gb, gb, wb, wb],
        out_specs=pl.BlockSpec((rows, nb), lambda j: (0, j)),
        out_shape=jax.ShapeDtypeStruct((rows, width), BF),
        cost_estimate=cost(
            4 * rows * width * n * ff, 4 * n * width * ff + 4 * rows * ff * n + 2 * rows * width
        ),
        name="input",
        **params(1),
    )(gg, gu, w_gate, w_up)


def after(a, *deps):
    return lax.optimization_barrier((a,) + deps)[0]


def body(tokens, grad_out, probs, expert_ids, serve_map, replica_pick, w_gate, w_up, w_down):
    groups = lax.axis_size("grp")
    columns = lax.axis_size("exp")
    devices = groups * columns
    planes = groups // 2
    half = columns // 2
    rows, width = tokens.shape
    top = expert_ids.shape[1]
    block = width // groups
    capacity = rows * top * 4 // (3 * devices)

    order = list(range(0, columns, 2)) + list(range(columns - 1, 0, -2))
    forward = [(order[i], order[(i + 1) % columns]) for i in range(columns)]
    backward = [(b, a) for a, b in forward]
    column = lax.axis_index("exp")
    position = jnp.where(column % 2 == 0, column // 2, columns - 1 - column // 2)
    offsets = [0]
    for s in range(1, half):
        offsets += [-s, s]
    offsets += [half]
    source = jnp.asarray(order, jnp.int32)[(position + jnp.asarray(offsets, jnp.int32)) % columns]

    def ring_step(s, f, b):
        if s < half:
            return lax.ppermute(f, "exp", forward), lax.ppermute(b, "exp", backward)
        h = f.shape[0] // 2
        return lax.ppermute(f[:h], "exp", forward), lax.ppermute(b[h:], "exp", backward)

    def tie(arrays, deps):
        n = len(arrays)
        return list(lax.optimization_barrier(tuple(arrays) + tuple(deps))[:n])

    def scatter_ring(a, waits):
        h = rows // 2
        at = {o: a[i * rows : (i + 1) * rows] for i, o in enumerate(offsets)}
        b, f = tie([at[half][:h], at[half][h:]], waits.get(1, []))
        b = lax.ppermute(b, "exp", backward)
        f = lax.ppermute(f, "exp", forward)
        for s in range(half - 1, 0, -1):
            mine_b, mine_f = at[-s].astype(F32), at[s].astype(F32)
            if s == half - 1:
                mine_b = jnp.concatenate([mine_b[:h] + b.astype(F32), mine_b[h:]], axis=0)
                mine_f = jnp.concatenate([mine_f[:h], mine_f[h:] + f.astype(F32)], axis=0)
            else:
                mine_b = mine_b + b.astype(F32)
                mine_f = mine_f + f.astype(F32)
            mine = [mine_b.astype(BF), mine_f.astype(BF)]
            mine_b, mine_f = tie(mine, waits.get(half + 1 - s, []))
            b = lax.ppermute(mine_b, "exp", backward)
            f = lax.ppermute(mine_f, "exp", forward)
        return (at[0].astype(F32) + b.astype(F32) + f.astype(F32)).astype(BF)

    group = lax.axis_index("grp")
    plane, core = group // 2, group % 2
    swap_core = [(g, g ^ 1) for g in range(groups)]

    w = width // planes
    doubled = jnp.concatenate([grad_out, grad_out], axis=1)
    rolled = lax.dynamic_slice_in_dim(doubled, (plane + 1) * w, width, axis=1)
    far, near = rolled[:, : width - w], rolled[:, width - w :]

    prob_expert, kept_route = routing(probs, expert_ids, serve_map, replica_pick, capacity)
    send = jnp.transpose(prob_expert, (1, 0, 2)).reshape(columns, rows * EXP_DEV).astype(BF)
    got = lax.all_to_all(send, "exp", split_axis=0, concat_axis=0, tiled=True)
    reorder = (source[:, None] == jnp.arange(columns, dtype=jnp.int32)[None, :]).astype(BF)
    prob_rows = dot(reorder, got, 1, 0).reshape(columns * rows, EXP_DEV)

    shift = {"x": 0, "far": 1, "near": half}
    first = {"x": tokens, "far": far, "near": near}
    arrived = {name: [a] for name, a in first.items()}
    hand = {name: [a, a] for name, a in first.items()}
    fresh = [tokens]
    hidden = []
    before = [send]
    for i in range(1, 2 * half + 1):
        names = [name for name in shift if 1 <= i - shift[name] <= half]
        moving = [a for name in names for a in hand[name]]
        if i > 1:
            moving = tie(moving, before)
        done = []
        for j, name in enumerate(names):
            hand[name] = ring_step(i - shift[name], *moving[2 * j : 2 * j + 2])
            arrived[name] += hand[name]
            done += hand[name]
            if name == "x":
                fresh += hand[name]
        before = done + (list(hidden[-1]) if i > 1 else [])
        if i == half:
            before += [prob_rows]
        if i < half - 1 or i == half:
            hidden.append(hidden_call(fresh, w_gate, w_up))
            fresh = []
    x_all, far_all, near_all = arrived["x"], arrived["far"], arrived["near"]
    hid, act, silu = [list(t) for t in zip(*hidden)]

    def part(s, lhs, which, rhs, p=None):
        start, pieces = lhs(s, which)
        return part_call(start, block, pieces, rhs, p)

    def to_core(a):
        return lax.ppermute(a, "grp", swap_core)

    def to_plane(s, a):
        return lax.ppermute(a, "grp", [(g, (g + 2 * s) % groups) for g in range(groups)])

    def of_x(s, which):
        return (((plane + s) % planes) * 2 + which) * block, x_all

    def of_far(s, which):
        return ((s - 1) * 2 + which) * block, far_all

    def of_near(s, which):
        return which * block, near_all

    def add(*arrays):
        return sum(a.astype(F32) for a in arrays)

    down = []
    free = []
    for s in range(1, planes):
        given = part(s, of_far, 1 - core, [hid], prob_rows)
        mine = part(s, of_far, core, [hid], prob_rows)
        got = to_core(given)
        for m in range(EXP_DEV):
            piece = add(mine[0, m], got[0, m]).astype(BF)
            if free:
                piece = after(piece, free[-1])
            else:
                plane_ref = after(plane.astype(jnp.int32).reshape(1), piece)
            free.append(to_plane(s, piece))
        down.append(free[-EXP_DEV:])

    gg, gu, prob_grad = back_call(
        plane_ref, far_all, near_all, w_down, prob_rows, hid, act, silu, planes
    )
    gg = after(gg, free[0])
    both = [[gg], [gu]]
    others = []
    chain = free[-1]
    for s in range(1, planes):
        given = part(s, of_x, 1 - core, both)
        mine = part(s, of_x, core, both)
        got = to_core(given)
        sums = []
        for i in range(2):
            for m in range(EXP_DEV):
                piece = add(mine[i, m], got[i, m]).astype(BF)
                chain = to_plane(s, after(piece, chain))
                sums.append(chain)
                if s == 1 and i == 0 and m == 0:
                    gg_x = after(gg, piece, free[-1])
        others.append(sums)
    first_sums = others[0]
    waits = {1: [first_sums[0]], half - 1: [first_sums[1]], half: [first_sums[2]]}
    grad_tokens = scatter_ring(input_call(gg_x, gu, w_gate, w_up), waits)

    given = part(0, of_x, 1 - core, both)
    mine = part(0, of_x, core, both)
    got = to_core(given)
    given_down = part(0, of_near, 1 - core, [hid], prob_rows)
    mine_down = part(0, of_near, core, [hid], prob_rows)
    got_down = to_core(given_down)

    def total(i, mine, got, theirs):
        return jnp.stack(
            [
                add(mine[i, m], got[i, m], *[t[i * EXP_DEV + m] for t in theirs])
                for m in range(EXP_DEV)
            ]
        )

    grad_down = total(0, mine_down, got_down, down)
    grad_gate = total(0, mine, got, others)
    grad_up = total(1, mine, got, others)

    ret = prob_grad.astype(BF).reshape(columns, rows * EXP_DEV)
    ret = dot(reorder, ret, 0, 0).astype(BF)
    ret = lax.all_to_all(ret, "exp", split_axis=0, concat_axis=0, tiled=True)
    ret = jnp.transpose(ret.reshape(columns, rows, EXP_DEV), (1, 0, 2)).reshape(rows, -1)
    pick = expert_ids[:, :, None] == jnp.arange(columns * EXP_DEV, dtype=jnp.int32)
    grad_probs = jnp.sum(jnp.where(pick, ret.astype(F32)[:, None, :], 0.0), axis=2)
    grad_probs = jnp.where(kept_route, grad_probs, 0.0).astype(BF)
    return (grad_tokens, grad_probs, grad_gate, grad_up, grad_down)


def solution(mesh):
    rows = P(("grp", "exp"), None)
    weights = P("exp", None, None)
    out = P("exp", "grp", None)
    return jax.shard_map(
        body,
        mesh=mesh,
        in_specs=(rows, rows, rows, rows, P(), rows, weights, weights, weights),
        out_specs=(rows, rows, out, out, out),
        check_vma=False,
    )
```

time: 520 us -> 287 us (0.55)
  waiting for transfers between devices: 240 us -> 60.9 us
  Pallas kernels: 0 us -> 131 us
  blocking collectives: 101 us -> 0 us
  matrix products: 51.2 us -> 0.64 us
  local copies, waits for them, and re-layouts: 47.4 us -> 9.02 us
  starting transfers between devices: 20 us -> 50.7 us
  between operations: 16.6 us -> 1.41 us
  other arithmetic: 39.8 us -> 33 us
    all_to_all x4 -> x2, waiting for transfers between devices: 173 us -> 1.5 us  [the longest x1 1.49 us: body(): ret = lax.all_to_all(ret, 'exp', split_axis=0, concat_axis=0, tiled=True)]
    pallas_call x0 -> x13, Pallas kernels: none -> 131 us  [the longest x8 60.6 us: part_call(): pl.pallas_call(functools.partial(part_kernel, len(pieces), row_counts, k,...]
    all_to_all x1 -> x0, blocking collectives: 101 us -> none  [body(): lax.all_to_all(input_send.reshape(devices, capacity, model_width), ('grp'...]
    reduce_scatter x3 -> x0, waiting for transfers between devices: 65.1 us -> none  [the longest x1 56.1 us: body(): lax.psum_scatter(spread(part_down).astype(jnp.bfloat16), 'grp', scatter_d...]
    ppermute x0 -> x42, waiting for transfers between devices: none -> 59.4 us  [the longest x6 25 us: to_plane(): lax.ppermute(a, 'grp', [(g, (g + 2 * s) % groups) for g in range(groups)])]
    dot_general x9 -> x3, matrix products: 51.2 us -> 0.64 us  [dot(): lax.dot_general(a, b, (((ca,), (cb,)), ((), ())), preferred_element_type=...]
    ppermute x0 -> x42, starting transfers between devices: none -> 42.5 us  [the longest x18 19.6 us: ring_step(): return (lax.ppermute(f, 'exp', forward), lax.ppermute(b, 'exp', backward))]
    gather x11 -> x1, local copies, waits for them, and re-layouts: 38 us -> 0.64 us  [body(): jnp.asarray(order, jnp.int32)]
  transfers between devices with their start and end apart: 7 -> 44, of which waited for: 4 -> 22; matrix products, arithmetic and copies ran while one was open for 16% -> 12% of each run, Pallas kernels for 0% -> 40%
where the time goes in v1:
time: 287 us; the launch traced here: 286 us
  Pallas kernels  131 us (46%)
  waiting for transfers between devices  60.9 us (21%)
  starting transfers between devices  50.7 us (18%)
  other arithmetic  33 us (11%)
  local copies, waits for them, and re-layouts  9.02 us (3%)
    pallas_call x8, Pallas kernels, part_call(): pl.pallas_call(functools.partial(part_kernel, len(pieces), row_counts, k,...  60.6 us
    pallas_call x3, Pallas kernels, hidden_call(): pl.pallas_call(functools.partial(hidden_kernel, len(pieces), nb), grid=(n...  34.6 us
    ppermute x6, waiting for transfers between devices, to_plane(): lax.ppermute(a, 'grp', [(g, (g + 2 * s) % groups) for g in range(groups)])  25 us
    ppermute x18, waiting for transfers between devices, ring_step(): return (lax.ppermute(f, 'exp', forward), lax.ppermute(b, 'exp', backward))  21.6 us
    ppermute x18, starting transfers between devices, ring_step(): return (lax.ppermute(f, 'exp', forward), lax.ppermute(b, 'exp', backward))  19.6 us
    pallas_call x1, Pallas kernels, input_call(): pl.pallas_call(input_kernel, grid=(width // nb,), in_specs=[gb, gb, wb, w...  18.6 us
    pallas_call x1, Pallas kernels, back_call(): pl.pallas_call(functools.partial(back_kernel, (len(pa), len(pb)), row_cou...  16.8 us
    another operation x4, other arithmetic, total(): jnp.stack([add(mine[i, m], got[i, m], *[t[i * EXP_DEV + m] for t in their...  9.46 us
  transfers between devices with their start and end apart: 44, of which 22 were waited for; matrix products, arithmetic and copies ran while one was open for 12% of the time, Pallas kernels for 40%

profile of v1, /device:TPU:0, one launch (start us, length us, event | category | flops | bytes accessed | tf_op | source)
XLA Modules:
  0.0 286.3 jit_solution(6783415075903068176)
XLA Ops:
  0.6 3.1 %collective-permute-start = (bf16[128,2048]{1,0:T(8,128)(2,1)}, bf16[128,2048]{1,0:T(8,128)(2,1)S(1)}, u32[]{:S(2)}, u32[]{:S(2)}) collective-permute-start(bf16[128,2048]{1,0:T(8,128)(2,1)} %refs_0_.9), channel_id=1, source_target_pairs={{0,2},{2,4},{4,6},{6,7},{7,5},{5,3},{3,1},{1,0},{8,10},{10,12},{12... | collective-permute-start | bytes 1572872 | tf_op jit(solution)/shard_map/ppermute | solution.py:313
  12.0 3.8 %collective-permute-done.refs_1_ = bf16[128,2048]{1,0:T(8,128)(2,1)S(1)} collective-permute-done((bf16[128,2048]{1,0:T(8,128)(2,1)}, bf16[128,2048]{1,0:T(8,128)(2,1)S(1)}, u32[]{:S(2)}, u32[]{:S(2)}) %collective-permute-start) | collective-permute-done | bytes 524320 | tf_op jit(solution)/shard_map/ppermute | solution.py:313
  21.3 4.8 %all-to-all-start = ((bf16[8,2,128]{2,1,0:T(2,128)(2,1)}), bf16[8,2,128]{2,1,0:T(2,128)(2,1)S(1)}, u32[]{:S(2)}, u32[]{:S(2)}) async-start(bf16[8,2,128]{2,1,0:T(2,128)(2,1)} %reshape.185), calls=%async_computation | async-start | bytes 8192 | tf_op jit(solution)/shard_map/all_to_all | solution.py:352
  28.2 12.2 %hidden.3 = (bf16[384,1536]{1,0:T(8,128)(2,1)}, bf16[384,1536]{1,0:T(8,128)(2,1)}, bf16[384,1536]{1,0:T(8,128)(2,1)}) custom-call(bf16[128,2048]{1,0:T(8,128)(2,1)} %refs_0_.9, bf16[128,2048]{1,0:T(8,128)(2,1)} %copy-done.6, bf16[128,2048]{1,0:T(8,128)(2,1)} %copy-done.7, bf16[2,2048,768]{2,1,0:T(8,128)(2,1)} %wg.1, bf16[2,2048,768]{2,1,0:T(8,128)(2,1)} %wu.1), custom_call_target="tpu_custom_call" | custom-call | flops 4831838208 | bytes 17301504 | tf_op jit(solution)/shard_map/hidden/pallas_call | solution.py:103
  44.7 10.1 %hidden.4 = (bf16[256,1536]{1,0:T(8,128)(2,1)}, bf16[256,1536]{1,0:T(8,128)(2,1)}, bf16[256,1536]{1,0:T(8,128)(2,1)}) custom-call(bf16[128,2048]{1,0:T(8,128)(2,1)} %copy-done.1, bf16[128,2048]{1,0:T(8,128)(2,1)} %copy-done.2, bf16[2,2048,768]{2,1,0:T(8,128)(2,1)} %wg.1, bf16[2,2048,768]{2,1,0:T(8,128)(2,1)} %wu.1), custom_call_target="tpu_custom_call" | custom-call | flops 3221225472 | bytes 15728640 | tf_op jit(solution)/shard_map/hidden/pallas_call | solution.py:103
  73.7 12.3 %hidden.5 = (bf16[384,1536]{1,0:T(8,128)(2,1)}, bf16[384,1536]{1,0:T(8,128)(2,1)}, bf16[384,1536]{1,0:T(8,128)(2,1)}) custom-call(bf16[128,2048]{1,0:T(8,128)(2,1)} %copy-done.4, bf16[128,2048]{1,0:T(8,128)(2,1)} %copy-done.5, bf16[64,2048]{1,0:T(8,128)(2,1)} %copy-done.9, bf16[64,2048]{1,0:T(8,128)(2,1)} %copy-done.10, bf16[2,2048,768]{2,1,0:T(8,128)(2,1)} %wg.1, ...), custom_call_target="tpu_custom_call" | custom-call | flops 4831838208 | bytes 17301504 | tf_op jit(solution)/shard_map/hidden/pallas_call | solution.py:103
  86.7 7.0 %part.9 = bf16[1,2,512,768]{3,2,1,0:T(8,128)(2,1)} custom-call(s32[1]{0:T(128)} %bitcast.5.start_ref, bf16[128,1024]{1,0:T(8,128)(2,1)} %copy-done.12, bf16[128,1024]{1,0:T(8,128)(2,1)} %copy-done.21, bf16[128,1024]{1,0:T(8,128)(2,1)} %copy-done.22, bf16[128,1024]{1,0:T(8,128)(2,1)} %copy-done.23, bf16[128,1024]{1,0:T(8,128)(2,1)} %collective-permute-done.7.refs_4_, ...), custom_call_target="tpu_custom_call" | custom-call | flops 1610612736 | bytes 7340032 | tf_op jit(solution)/shard_map/part/pallas_call | solution.py:232
  95.8 6.6 %collective-permute-done.17.refs_10_.refs_1_ = bf16[128,1024]{1,0:T(8,128)(2,1)S(1)} collective-permute-done((bf16[128,1024]{1,0:T(8,128)(2,1)S(1)}, bf16[128,1024]{1,0:T(8,128)(2,1)S(1)}, u32[]{:S(2)}, u32[]{:S(2)}) %collective-permute-start.17) | collective-permute-done | bytes 262176 | tf_op jit(solution)/shard_map/ppermute | solution.py:313
  106.2 7.0 %part.8 = bf16[1,2,512,768]{3,2,1,0:T(8,128)(2,1)} custom-call(s32[1]{0:T(128)} %bitcast.1.start_ref, bf16[128,1024]{1,0:T(8,128)(2,1)} %copy-done.12, bf16[128,1024]{1,0:T(8,128)(2,1)} %copy-done.21, bf16[128,1024]{1,0:T(8,128)(2,1)} %copy-done.22, bf16[128,1024]{1,0:T(8,128)(2,1)} %copy-done.23, bf16[128,1024]{1,0:T(8,128)(2,1)} %collective-permute-done.7.refs_4_, ...), custom_call_target="tpu_custom_call" | custom-call | flops 1610612736 | bytes 7340032 | tf_op jit(solution)/shard_map/part/pallas_call | solution.py:232
  128.4 16.8 %back.1 = (bf16[1024,1536]{1,0:T(8,128)(2,1)}, bf16[1024,1536]{1,0:T(8,128)(2,1)}, f32[1024,2]{1,0:T(8,128)}) custom-call(s32[1]{0:T(128)} %bitcast.plane_ref, bf16[128,1024]{1,0:T(8,128)(2,1)} %copy-done.12, bf16[128,1024]{1,0:T(8,128)(2,1)} %copy-done.21, bf16[128,1024]{1,0:T(8,128)(2,1)} %copy-done.22, bf16[128,1024]{1,0:T(8,128)(2,1)} %copy-done.23, ...), custom_call_target="tpu_custom_call" | custom-call | flops 6442450944 | bytes 28311552 | tf_op jit(solution)/shard_map/back/pallas_call | solution.py:166
  146.1 8.2 %part.11 = bf16[2,2,512,768]{3,2,1,0:T(8,128)(2,1)} custom-call(s32[1]{0:T(128)} %bitcast.9.start_ref, bf16[128,2048]{1,0:T(8,128)(2,1)} %refs_0_.9, bf16[128,2048]{1,0:T(8,128)(2,1)} %copy-done.6, bf16[128,2048]{1,0:T(8,128)(2,1)} %copy-done.7, bf16[128,2048]{1,0:T(8,128)(2,1)} %copy-done.1, bf16[128,2048]{1,0:T(8,128)(2,1)} %copy-done.2, ...), custom_call_target="tpu_custom_call" | custom-call | flops 3221225472 | bytes 13631488 | tf_op jit(solution)/shard_map/part/pallas_call | solution.py:232
  156.0 7.0 %part.15 = bf16[1,2,512,768]{3,2,1,0:T(8,128)(2,1)} custom-call(s32[1]{0:T(128)} %bitcast.5.start_ref, bf16[128,1024]{1,0:T(8,128)(2,1)} %copy-done.11, bf16[128,1024]{1,0:T(8,128)(2,1)} %copy-done.17, bf16[128,1024]{1,0:T(8,128)(2,1)} %copy-done.18, bf16[128,1024]{1,0:T(8,128)(2,1)} %copy-done.19, bf16[128,1024]{1,0:T(8,128)(2,1)} %copy-done.20, ...), custom_call_target="tpu_custom_call" | custom-call | flops 1610612736 | bytes 7340032 | tf_op jit(solution)/shard_map/part/pallas_call | solution.py:232
  163.5 8.2 %part.10 = bf16[2,2,512,768]{3,2,1,0:T(8,128)(2,1)} custom-call(s32[1]{0:T(128)} %bitcast.8.start_ref, bf16[128,2048]{1,0:T(8,128)(2,1)} %refs_0_.9, bf16[128,2048]{1,0:T(8,128)(2,1)} %copy-done.6, bf16[128,2048]{1,0:T(8,128)(2,1)} %copy-done.7, bf16[128,2048]{1,0:T(8,128)(2,1)} %copy-done.1, bf16[128,2048]{1,0:T(8,128)(2,1)} %copy-done.2, ...), custom_call_target="tpu_custom_call" | custom-call | flops 3221225472 | bytes 13631488 | tf_op jit(solution)/shard_map/part/pallas_call | solution.py:232
  171.7 3.7 %fusion.13 = (bf16[512,768]{1,0:T(8,128)(2,1)}, bf16[512,768]{1,0:T(8,128)(2,1)}, bf16[512,768]{1,0:T(8,128)(2,1)}, bf16[512,768]{1,0:T(8,128)(2,1)S(1)}) fusion(bf16[2,2,512,768]{3,2,1,0:T(8,128)(2,1)S(1)} %collective-permute-done.26, bf16[2,2,512,768]{3,2,1,0:T(8,128)(2,1)} %part.10), kind=kLoop, calls=%fused_computation.38 | loop fusion | flops 6291456 | bytes 9437184 | tf_op jit(solution)/shard_map/convert_element_type | solution.py:435
  176.1 18.6 %input.1 = bf16[1024,2048]{1,0:T(8,128)(2,1)} custom-call(bf16[1024,1536]{1,0:T(8,128)(2,1)} %get-tuple-element.91.refs_9_.gg, bf16[1024,1536]{1,0:T(8,128)(2,1)} %get-tuple-element.89.refs_10_.gu, bf16[2,2048,768]{2,1,0:T(8,128)(2,1)} %wg.1, bf16[2,2048,768]{2,1,0:T(8,128)(2,1)} %wu.1), custom_call_target="tpu_custom_call" | custom-call | flops 12884901888 | bytes 23068672 | tf_op jit(solution)/shard_map/input/pallas_call | solution.py:271
  198.1 8.2 %part.13 = bf16[2,2,512,768]{3,2,1,0:T(8,128)(2,1)} custom-call(s32[1]{0:T(128)} %bitcast.19.start_ref, bf16[128,2048]{1,0:T(8,128)(2,1)} %refs_0_.9, bf16[128,2048]{1,0:T(8,128)(2,1)} %copy-done.6, bf16[128,2048]{1,0:T(8,128)(2,1)} %copy-done.7, bf16[128,2048]{1,0:T(8,128)(2,1)} %copy-done.1, bf16[128,2048]{1,0:T(8,128)(2,1)} %copy-done.2, ...), custom_call_target="tpu_custom_call" | custom-call | flops 3221225472 | bytes 13631488 | tf_op jit(solution)/shard_map/part/pallas_call | solution.py:232
  212.1 3.3 %all-to-all-start.1 = ((bf16[8,2,128]{2,1,0:T(2,128)(2,1)}), bf16[8,2,128]{2,1,0:T(2,128)(2,1)S(1)}, u32[]{:S(2)}, u32[]{:S(2)}) async-start(bf16[8,2,128]{2,1,0:T(2,128)(2,1)} %reshape.187), calls=%async_computation.1 | async-start | bytes 8192 | tf_op jit(solution)/shard_map/all_to_all | solution.py:466
  215.4 7.0 %part.14 = bf16[1,2,512,768]{3,2,1,0:T(8,128)(2,1)} custom-call(s32[1]{0:T(128)} %bitcast.1.start_ref, bf16[128,1024]{1,0:T(8,128)(2,1)} %copy-done.11, bf16[128,1024]{1,0:T(8,128)(2,1)} %copy-done.17, bf16[128,1024]{1,0:T(8,128)(2,1)} %copy-done.18, bf16[128,1024]{1,0:T(8,128)(2,1)} %copy-done.19, bf16[128,1024]{1,0:T(8,128)(2,1)} %copy-done.20, ...), custom_call_target="tpu_custom_call" | custom-call | flops 1610612736 | bytes 7340032 | tf_op jit(solution)/shard_map/part/pallas_call | solution.py:232
  227.5 15.6 %collective-permute-done.33 = bf16[512,768]{1,0:T(8,128)(2,1)} collective-permute-done((bf16[512,768]{1,0:T(8,128)(2,1)}, bf16[512,768]{1,0:T(8,128)(2,1)}, u32[]{:S(2)}, u32[]{:S(2)}) %collective-permute-start.33) | collective-permute-done | bytes 786464 | tf_op jit(solution)/shard_map/ppermute | solution.py:392
  247.0 8.2 %part.12 = bf16[2,2,512,768]{3,2,1,0:T(8,128)(2,1)} custom-call(s32[1]{0:T(128)} %bitcast.18.start_ref, bf16[128,2048]{1,0:T(8,128)(2,1)} %refs_0_.9, bf16[128,2048]{1,0:T(8,128)(2,1)} %copy-done.6, bf16[128,2048]{1,0:T(8,128)(2,1)} %copy-done.7, bf16[128,2048]{1,0:T(8,128)(2,1)} %copy-done.1, bf16[128,2048]{1,0:T(8,128)(2,1)} %copy-done.2, ...), custom_call_target="tpu_custom_call" | custom-call | flops 3221225472 | bytes 13631488 | tf_op jit(solution)/shard_map/part/pallas_call | solution.py:232
  258.1 5.0 %collective-permute-done.36 = bf16[512,768]{1,0:T(8,128)(2,1)S(1)} collective-permute-done((bf16[512,768]{1,0:T(8,128)(2,1)S(1)}, bf16[512,768]{1,0:T(8,128)(2,1)S(1)}, u32[]{:S(2)}, u32[]{:S(2)}) %collective-permute-start.36) | collective-permute-done | bytes 786464 | tf_op jit(solution)/shard_map/ppermute | solution.py:392
  270.5 3.4 %collective-permute-done.38 = bf16[128,2048]{1,0:T(8,128)(2,1)S(1)} collective-permute-done((bf16[128,2048]{1,0:T(8,128)(2,1)S(1)}, bf16[128,2048]{1,0:T(8,128)(2,1)S(1)}, u32[]{:S(2)}, u32[]{:S(2)}) %collective-permute-start.38) | collective-permute-done | bytes 524320 | tf_op jit(solution)/shard_map/ppermute | solution.py:338
  276.5 4.5 %collective-permute-done.40 = bf16[512,768]{1,0:T(8,128)(2,1)S(1)} collective-permute-done((bf16[512,768]{1,0:T(8,128)(2,1)S(1)}, bf16[512,768]{1,0:T(8,128)(2,1)S(1)}, u32[]{:S(2)}, u32[]{:S(2)}) %collective-permute-start.40) | collective-permute-done | bytes 786464 | tf_op jit(solution)/shard_map/ppermute | solution.py:392
  283.1 3.2 %pad_maximum_fusion = (f32[2,512,768]{2,1,0:T(8,128)}, f32[2,512,768]{2,1,0:T(8,128)}) fusion(f32[1,512,768]{2,1,0:T(8,128)S(1)} %get-tuple-element.111, f32[1,512,768]{2,1,0:T(8,128)S(1)} %get-tuple-element.112, f32[1,512,768]{2,1,0:T(8,128)S(1)} %get-tuple-element.110, f32[1,512,768]{2,1,0:T(8,128)S(1)} %get-tuple-element.109), kind=kLoop, calls=%fused_computation.1 | loop fusion | flops 1572864 | bytes 12582912 | tf_op jit(solution)/shard_map/stack | solution.py:453
  (208 shorter events, 97.3 us)
Async XLA Ops:
  0.6 15.2 %collective-permute-start = (bf16[128,2048]{1,0:T(8,128)(2,1)}, bf16[128,2048]{1,0:T(8,128)(2,1)S(1)}, u32[]{:S(2)}, u32[]{:S(2)}) collective-permute-start(bf16[128,2048]{1,0:T(8,128)(2,1)} %refs_0_.9), channel_id=1, source_target_pairs={{0,2},{2,4},{4,6},{6,7},{7,5},{5,3},{3,1},{1,0},{8,10},{10,12},{12... | collective-permute-start | bytes 1572872 | tf_op jit(solution)/shard_map/ppermute | solution.py:313
  3.7 13.6 %collective-permute-start.1 = (bf16[128,2048]{1,0:T(8,128)(2,1)}, bf16[128,2048]{1,0:T(8,128)(2,1)S(1)}, u32[]{:S(2)}, u32[]{:S(2)}) collective-permute-start(bf16[128,2048]{1,0:T(8,128)(2,1)} %refs_0_.9), channel_id=1, source_target_pairs={{2,0},{4,2},{6,4},{7,6},{5,7},{3,5},{1,3},{0,1},{10,8},{12,10},{14... | collective-permute-start | bytes 1572872 | tf_op jit(solution)/shard_map/ppermute | solution.py:313
  17.3 23.2 %collective-permute-start.4 = (bf16[128,2048]{1,0:T(8,128)(2,1)S(1)}, bf16[128,2048]{1,0:T(8,128)(2,1)S(1)}, u32[]{:S(2)}, u32[]{:S(2)}) collective-permute-start(bf16[128,2048]{1,0:T(8,128)(2,1)S(1)} %collective-permute-done.refs_1_), channel_id=1, source_target_pairs={{0,2},{2,4},{4,6},{6,7},{7,5},{5,3},{3,1},{1,0},{8,10},{10,12},{12... | collective-permute-start | bytes 1572872 | tf_op jit(solution)/shard_map/ppermute | solution.py:313
  18.9 21.7 %collective-permute-start.5 = (bf16[128,2048]{1,0:T(8,128)(2,1)S(1)}, bf16[128,2048]{1,0:T(8,128)(2,1)S(1)}, u32[]{:S(2)}, u32[]{:S(2)}) collective-permute-start(bf16[128,2048]{1,0:T(8,128)(2,1)S(1)} %collective-permute-done.1.refs_2_), channel_id=1, source_target_pairs={{2,0},{4,2},{6,4},{7,6},{5,7},{3,5},{1,3},{0,1},{10,8},{12,10},{14... | collective-permute-start | bytes 1572872 | tf_op jit(solution)/shard_map/ppermute | solution.py:313
  21.3 42.5 %all-to-all-start = ((bf16[8,2,128]{2,1,0:T(2,128)(2,1)}), bf16[8,2,128]{2,1,0:T(2,128)(2,1)S(1)}, u32[]{:S(2)}, u32[]{:S(2)}) async-start(bf16[8,2,128]{2,1,0:T(2,128)(2,1)} %reshape.185), calls=%async_computation | async-start | bytes 8192 | tf_op jit(solution)/shard_map/all_to_all | solution.py:352
  26.1 14.3 %collective-permute-start.2 = (bf16[128,1024]{1,0:T(8,128)(2,1)S(1)}, bf16[128,1024]{1,0:T(8,128)(2,1)S(1)}, u32[]{:S(2)}, u32[]{:S(2)}) collective-permute-start(bf16[128,1024]{1,0:T(8,128)(2,1)S(1)} %get-tuple-element.56.refs_0_), channel_id=1, source_target_pairs={{0,2},{2,4},{4,6},{6,7},{7,5},{5,3},{3,1},{1,0},{8,10},{10,12},{12... | collective-permute-start | bytes 786440 | tf_op jit(solution)/shard_map/ppermute | solution.py:313
  40.6 18.4 %collective-permute-start.8 = (bf16[128,2048]{1,0:T(8,128)(2,1)S(1)}, bf16[128,2048]{1,0:T(8,128)(2,1)S(1)}, u32[]{:S(2)}, u32[]{:S(2)}) collective-permute-start(bf16[128,2048]{1,0:T(8,128)(2,1)S(1)} %collective-permute-done.4.refs_0_.refs_3_), channel_id=1, source_target_pairs={{0,2},{2,4},{4,6},{6,7},{7,5},{5,3},{3,1},{1,0},{8,10},{10,12},{12... | collective-permute-start | bytes 1572872 | tf_op jit(solution)/shard_map/ppermute | solution.py:313
  42.6 16.4 %collective-permute-start.9 = (bf16[128,2048]{1,0:T(8,128)(2,1)S(1)}, bf16[128,2048]{1,0:T(8,128)(2,1)S(1)}, u32[]{:S(2)}, u32[]{:S(2)}) collective-permute-start(bf16[128,2048]{1,0:T(8,128)(2,1)S(1)} %collective-permute-done.5.refs_1_.refs_4_), channel_id=1, source_target_pairs={{2,0},{4,2},{6,4},{7,6},{5,7},{3,5},{1,3},{0,1},{10,8},{12,10},{14... | collective-permute-start | bytes 1572872 | tf_op jit(solution)/shard_map/ppermute | solution.py:313
  42.7 14.7 %collective-permute-start.6 = (bf16[128,1024]{1,0:T(8,128)(2,1)S(1)}, bf16[128,1024]{1,0:T(8,128)(2,1)S(1)}, u32[]{:S(2)}, u32[]{:S(2)}) collective-permute-start(bf16[128,1024]{1,0:T(8,128)(2,1)S(1)} %collective-permute-done.2.refs_1_), channel_id=1, source_target_pairs={{0,2},{2,4},{4,6},{6,7},{7,5},{5,3},{3,1},{1,0},{8,10},{10,12},{12... | collective-permute-start | bytes 786440 | tf_op jit(solution)/shard_map/ppermute | solution.py:313
  44.7 14.3 %collective-permute-start.7 = (bf16[128,1024]{1,0:T(8,128)(2,1)S(1)}, bf16[128,1024]{1,0:T(8,128)(2,1)}, u32[]{:S(2)}, u32[]{:S(2)}) collective-permute-start(bf16[128,1024]{1,0:T(8,128)(2,1)S(1)} %collective-permute-done.3.refs_2_), channel_id=1, source_target_pairs={{2,0},{4,2},{6,4},{7,6},{5,7},{3,5},{1,3},{0,1},{10,8},{12,10},{14... | collective-permute-start | bytes 786440 | tf_op jit(solution)/shard_map/ppermute | solution.py:313
  71.4 14.6 %collective-permute-start.14 = (bf16[64,1024]{1,0:T(8,128)(2,1)S(1)}, bf16[64,1024]{1,0:T(8,128)(2,1)S(1)}, u32[]{:S(2)}, u32[]{:S(2)}) collective-permute-start(bf16[64,1024]{1,0:T(8,128)(2,1)S(1)} %slice.150), channel_id=1, source_target_pairs={{0,2},{2,4},{4,6},{6,7},{7,5},{5,3},{3,1},{1,0},{8,10},{10,12},{12... | collective-permute-start | bytes 393224 | tf_op jit(solution)/shard_map/ppermute | solution.py:315
  73.1 12.9 %collective-permute-start.15 = (bf16[64,1024]{1,0:T(8,128)(2,1)S(1)}, bf16[64,1024]{1,0:T(8,128)(2,1)S(1)}, u32[]{:S(2)}, u32[]{:S(2)}) collective-permute-start(bf16[64,1024]{1,0:T(8,128)(2,1)S(1)} %slice.151), channel_id=1, source_target_pairs={{2,0},{4,2},{6,4},{7,6},{5,7},{3,5},{1,3},{0,1},{10,8},{12,10},{14... | collective-permute-start | bytes 393224 | tf_op jit(solution)/shard_map/ppermute | solution.py:315
  93.7 21.6 %collective-permute-start.16 = (bf16[1,2,512,768]{3,2,1,0:T(8,128)(2,1)}, bf16[1,2,512,768]{3,2,1,0:T(8,128)(2,1)S(1)}, u32[]{:S(2)}, u32[]{:S(2)}) collective-permute-start(bf16[1,2,512,768]{3,2,1,0:T(8,128)(2,1)} %part.9), channel_id=1, source_target_pairs={{0,8},{8,0},{16,24},{24,16},{1,9},{9,1},{17,25},{25,17},{2,10},{10... | collective-permute-start | bytes 4718600 | tf_op jit(solution)/shard_map/ppermute | solution.py:389
  118.2 27.0 %collective-permute-start.25 = (bf16[512,768]{1,0:T(8,128)(2,1)}, bf16[512,768]{1,0:T(8,128)(2,1)S(1)}, u32[]{:S(2)}, u32[]{:S(2)}) collective-permute-start(bf16[512,768]{1,0:T(8,128)(2,1)} %get-tuple-element.130), channel_id=1, source_target_pairs={{0,16},{8,24},{16,0},{24,8},{1,17},{9,25},{17,1},{25,9},{2,18},{10... | collective-permute-start | bytes 2359304 | tf_op jit(solution)/shard_map/ppermute | solution.py:392
  154.3 17.4 %collective-permute-start.26 = (bf16[2,2,512,768]{3,2,1,0:T(8,128)(2,1)}, bf16[2,2,512,768]{3,2,1,0:T(8,128)(2,1)S(1)}, u32[]{:S(2)}, u32[]{:S(2)}) collective-permute-start(bf16[2,2,512,768]{3,2,1,0:T(8,128)(2,1)} %part.11), channel_id=1, source_target_pairs={{0,8},{8,0},{16,24},{24,16},{1,9},{9,1},{17,25},{25,17},{2,10},{10... | collective-permute-start | bytes 9437192 | tf_op jit(solution)/shard_map/ppermute | solution.py:389
  154.5 20.9 %collective-permute-start.27 = (bf16[512,768]{1,0:T(8,128)(2,1)}, bf16[512,768]{1,0:T(8,128)(2,1)}, u32[]{:S(2)}, u32[]{:S(2)}) collective-permute-start(bf16[512,768]{1,0:T(8,128)(2,1)} %get-tuple-element.90), channel_id=1, source_target_pairs={{0,16},{8,24},{16,0},{24,8},{1,17},{9,25},{17,1},{25,9},{2,18},{10... | collective-permute-start | bytes 2359304 | tf_op jit(solution)/shard_map/ppermute | solution.py:392
  163.0 103.3 %collective-permute-start.41 = (bf16[1,2,512,768]{3,2,1,0:T(8,128)(2,1)}, bf16[1,2,512,768]{3,2,1,0:T(8,128)(2,1)}, u32[]{:S(2)}, u32[]{:S(2)}) collective-permute-start(bf16[1,2,512,768]{3,2,1,0:T(8,128)(2,1)} %part.15), channel_id=1, source_target_pairs={{0,8},{8,0},{16,24},{24,16},{1,9},{9,1},{17,25},{25,17},{2,10},{10... | collective-permute-start | bytes 4718600 | tf_op jit(solution)/shard_map/ppermute | solution.py:389
  175.4 20.6 %collective-permute-start.28 = (bf16[512,768]{1,0:T(8,128)(2,1)S(1)}, bf16[512,768]{1,0:T(8,128)(2,1)S(1)}, u32[]{:S(2)}, u32[]{:S(2)}) collective-permute-start(bf16[512,768]{1,0:T(8,128)(2,1)S(1)} %get-tuple-element.92), channel_id=1, source_target_pairs={{0,16},{8,24},{16,0},{24,8},{1,17},{9,25},{17,1},{25,9},{2,18},{10... | collective-permute-start | bytes 2359304 | tf_op jit(solution)/shard_map/ppermute | solution.py:392
  206.3 70.2 %collective-permute-start.39 = (bf16[2,2,512,768]{3,2,1,0:T(8,128)(2,1)}, bf16[2,2,512,768]{3,2,1,0:T(8,128)(2,1)S(1)}, u32[]{:S(2)}, u32[]{:S(2)}) collective-permute-start(bf16[2,2,512,768]{3,2,1,0:T(8,128)(2,1)} %part.13), channel_id=1, source_target_pairs={{0,8},{8,0},{16,24},{24,16},{1,9},{9,1},{17,25},{25,17},{2,10},{10... | collective-permute-start | bytes 9437192 | tf_op jit(solution)/shard_map/ppermute | solution.py:389
  208.6 16.9 %collective-permute-start.32 = (bf16[128,2048]{1,0:T(8,128)(2,1)}, bf16[128,2048]{1,0:T(8,128)(2,1)}, u32[]{:S(2)}, u32[]{:S(2)}) collective-permute-start(bf16[128,2048]{1,0:T(8,128)(2,1)} %get-tuple-element.96), channel_id=1, source_target_pairs={{0,2},{2,4},{4,6},{6,7},{7,5},{5,3},{3,1},{1,0},{8,10},{10,12},{12... | collective-permute-start | bytes 1572872 | tf_op jit(solution)/shard_map/ppermute | solution.py:338
  209.3 16.2 %collective-permute-start.31 = (bf16[128,2048]{1,0:T(8,128)(2,1)}, bf16[128,2048]{1,0:T(8,128)(2,1)}, u32[]{:S(2)}, u32[]{:S(2)}) collective-permute-start(bf16[128,2048]{1,0:T(8,128)(2,1)} %get-tuple-element.95), channel_id=1, source_target_pairs={{2,0},{4,2},{6,4},{7,6},{5,7},{3,5},{1,3},{0,1},{10,8},{12,10},{14... | collective-permute-start | bytes 1572872 | tf_op jit(solution)/shard_map/ppermute | solution.py:337
  224.0 19.1 %collective-permute-start.33 = (bf16[512,768]{1,0:T(8,128)(2,1)}, bf16[512,768]{1,0:T(8,128)(2,1)}, u32[]{:S(2)}, u32[]{:S(2)}) collective-permute-start(bf16[512,768]{1,0:T(8,128)(2,1)} %get-tuple-element.97), channel_id=1, source_target_pairs={{0,16},{8,24},{16,0},{24,8},{1,17},{9,25},{17,1},{25,9},{2,18},{10... | collective-permute-start | bytes 2359304 | tf_op jit(solution)/shard_map/ppermute | solution.py:392
  245.7 17.3 %collective-permute-start.36 = (bf16[512,768]{1,0:T(8,128)(2,1)S(1)}, bf16[512,768]{1,0:T(8,128)(2,1)S(1)}, u32[]{:S(2)}, u32[]{:S(2)}) collective-permute-start(bf16[512,768]{1,0:T(8,128)(2,1)S(1)} %copy-done.25), channel_id=1, source_target_pairs={{0,16},{8,24},{16,0},{24,8},{1,17},{9,25},{17,1},{25,9},{2,18},{10... | collective-permute-start | bytes 2359304 | tf_op jit(solution)/shard_map/ppermute | solution.py:392
  265.1 15.8 %collective-permute-start.40 = (bf16[512,768]{1,0:T(8,128)(2,1)S(1)}, bf16[512,768]{1,0:T(8,128)(2,1)S(1)}, u32[]{:S(2)}, u32[]{:S(2)}) collective-permute-start(bf16[512,768]{1,0:T(8,128)(2,1)S(1)} %copy-done.24), channel_id=1, source_target_pairs={{0,16},{8,24},{16,0},{24,8},{1,17},{9,25},{17,1},{25,9},{2,18},{10... | collective-permute-start | bytes 2359304 | tf_op jit(solution)/shard_map/ppermute | solution.py:392
  (57 other events, 642.4 us)
